TPU v7x, 128 devices: a whole 4x4x4 slice. The times are simulated.
128 devices in a mesh: dp: 16 (over x, z_lo, core), vocab: 8 (over y, z_hi).
Axes of the slice: x: 4, y: 4, z: 4 (z_hi: 2, z_lo: 2; z = z_hi * 2 + z_lo), core: 2. Of those that a mesh axis runs over, the one named last changes fastest.
Arguments:
- hidden_states: bfloat16 [32768, 4096], P('dp'), may hold values from -6 to 6
- logit_grads: bfloat16 [32768, 12288], P('dp', 'vocab'), may hold values from -0.03125 to 0.03125
- master: float32 [8, 1536, 4096], P('vocab', 'dp'), may hold values from -0.006 to 0.006
- moment_one: float32 [8, 1536, 4096], P('vocab', 'dp'), may hold values from -4 to 4
- moment_two: float32 [8, 1536, 4096], P('vocab', 'dp'), may hold values from 0.0001 to 0.01
Outputs:
- new_master: float32 [8, 1536, 4096], P('vocab', 'dp')
- new_moment_one: float32 [8, 1536, 4096], P('vocab', 'dp')
- new_moment_two: float32 [8, 1536, 4096], P('vocab', 'dp')
- sampler_head: bfloat16 [12288, 4096], P(None, 'vocab')
All inputs are finite; a program needn't handle non-finite values.
Results may differ from a plain program's by a relative error of at most 0.001.
Values may be sent and summed in bfloat16 or wider, within the bound.
No kernel may reach another device: no remote copies, remote signals or barrier semaphores. Data moves between devices by JAX's collectives and lax.ppermute only.
A program may use at most 192 MiB of HBM per device.

v0:
```python
import jax
import jax.numpy as jnp
from jax import lax
from jax.sharding import PartitionSpec as P

STEP = 100


beta_one = 0.9
beta_two = 0.999
learn_rate = 0.001
decay_rate = 0.1
epsilon = 1e-08


def local(hidden_states, logit_grads, master, moment_one, moment_two):
    gradient = lax.psum_scatter(
        lax.dot_general(
            logit_grads, hidden_states, (((0,), (0,)), ((), ())), preferred_element_type=jnp.float32
        ),
        "dp",
        scatter_dimension=0,
        tiled=True,
    )
    gradient = gradient[None]
    new_moment_one = beta_one * moment_one + (1.0 - beta_one) * gradient
    new_moment_two = beta_two * moment_two + (1.0 - beta_two) * gradient * gradient
    first_hat = new_moment_one / (1.0 - beta_one**STEP)
    second_hat = new_moment_two / (1.0 - beta_two**STEP)
    new_master = master - learn_rate * (
        first_hat / (jnp.sqrt(second_hat) + epsilon) + decay_rate * master
    )
    rounded = new_master.astype(jnp.bfloat16)
    copies = lax.all_gather(rounded, "dp", axis=1, tiled=True)
    sampler = lax.all_to_all(copies, "vocab", split_axis=2, concat_axis=0, tiled=True)
    sampler_head = sampler.reshape(sampler.shape[0] * sampler.shape[1], sampler.shape[2])
    return (new_master, new_moment_one, new_moment_two, sampler_head)


def solution(mesh):
    in_specs = (
        P("dp", None),
        P("dp", "vocab"),
        P("vocab", "dp", None),
        P("vocab", "dp", None),
        P("vocab", "dp", None),
    )
    out_specs = (
        P("vocab", "dp", None),
        P("vocab", "dp", None),
        P("vocab", "dp", None),
        P(None, "vocab"),
    )
    return jax.shard_map(local, mesh=mesh, in_specs=in_specs, out_specs=out_specs, check_vma=False)
```

profile of v0, /device:TPU:1, one launch (start us, length us, event | category | flops | bytes accessed | tf_op | source)
XLA Modules:
  0.0 743.3 jit_solution(12478472355489560168)
XLA Ops:
  7.2 0.0 reduce-scatter.2.cloned.1.call-start
  7.2 33.7 %fusion.4 = f32[1536,4096]{1,0:T(8,128)} fusion(bf16[2048,1536]{1,0:T(8,128)(2,1)} %param.6, bf16[2048,4096]{1,0:T(8,128)(2,1)} %param.5), kind=kOutput, calls=%fused_computation.6 | convolution fusion | flops 25769803776 | bytes 48234496 | tf_op jit(solution)/shard_map/dot_general | solution.py:18
  40.9 0.0 copy-start
  40.9 0.0 copy-start.1
  40.9 0.0 reduce-scatter.2.cloned.1.call-update
  40.9 0.2 all-gather.2.cloned.1.call-start
  41.1 268.5 %reduce-scatter.2.cloned.1.call-done = f32[96,4096]{1,0:T(8,128)} async-done(((f32[1536,4096]{1,0:T(8,128)}), f32[96,4096]{1,0:T(8,128)}) %reduce-scatter.2.cloned.1.call-update) | async-done | bytes 1572880 | tf_op jit(solution)/shard_map/reduce_scatter | solution.py:17
  309.7 0.0 copy-done
  309.7 0.0 copy-done.1
  309.7 5.2 fusion.2
  314.8 0.0 all-gather.2.cloned.1.call-update
  314.9 72.5 %all-gather.2.cloned.1.call-done = bf16[1,1536,4096]{2,1,0:T(8,128)(2,1)} async-done(((bf16[1,96,4096]{2,1,0:T(8,128)(2,1)}), bf16[1,1536,4096]{2,1,0:T(8,128)(2,1)}) %all-gather.2.cloned.1.call-update) | async-done | bytes 12582928 | tf_op jit(solution)/shard_map/all_gather | solution.py:34
  387.4 54.8 %copy.13 = bf16[1,1536,4096]{1,0,2:T(2,128)(2,1)} copy(bf16[1,1536,4096]{2,1,0:T(8,128)(2,1)} %all-gather.2.cloned.1.call-done) | data formatting | bytes 25165824 | tf_op jit(solution)/shard_map/all_gather | solution.py:34
  442.2 0.6 broadcast.26
  442.7 81.3 %reduce = bf16[4096,1536]{1,0:T(8,128)(2,1)} reduce(bf16[4096,1,1536]{2,1,0:T(2,128)(2,1)} %bitcast.16, bf16[]{:T(256)} %broadcast.26), dimensions={1}, to_apply=%bitcast.10.reduce_sub_computation | reduce | bytes 25165826
  524.0 14.5 %reshape.16 = bf16[8,2,393216]{2,1,0:T(2,128)(2,1)} reshape(bf16[4096,1536]{1,0:T(8,128)(2,1)} %reduce) | data formatting | bytes 25165824
  538.5 147.0 %all_to_all.15 = bf16[8,2,393216]{2,1,0:T(2,128)(2,1)} all-to-all(bf16[8,2,393216]{2,1,0:T(2,128)(2,1)} %reshape.16), channel_id=1, replica_groups=mesh['dp'=16,'vocab'=8] {'vocab'}, dimensions={0} | all-to-all | bytes 25165824 | tf_op jit(solution)/shard_map/all_to_all | solution.py:35
  685.5 17.9 %reshape.17 = bf16[4096,1,1536]{2,1,0:T(2,128)(2,1)} reshape(bf16[8,2,393216]{2,1,0:T(2,128)(2,1)} %all_to_all.15) | data formatting | bytes 25165824
  703.4 16.4 %copy.15 = bf16[1,1536,4096]{1,2,0:T(8,128)(2,1)} copy(bf16[1,1536,4096]{1,0,2:T(2,128)(2,1)} %bitcast.17) | data formatting | bytes 25165824
  719.8 16.6 %copy.14 = bf16[8,1,1536,512]{3,2,0,1:T(8,128)(2,1)} copy(bf16[8,1,1536,512]{2,3,0,1:T(8,128)(2,1)} %bitcast.18) | data formatting | bytes 25165824 | tf_op jit(solution)/shard_map/all_to_all | solution.py:35
Async XLA Ops:
  7.2 302.5 %reduce-scatter.2.cloned.1.call-start = ((), (), s32[]{:S(2)}) async-start(), calls=%async_computation.2 | async-start | bytes 26738688 | tf_op jit(solution)/shard_map/reduce_scatter | solution.py:17
  40.9 268.8 %copy-start = (f32[1,96,4096]{2,1,0:T(8,128)S(1)}, f32[1,96,4096]{2,1,0:T(8,128)}, u32[]{:S(2)}) copy-start(f32[1,96,4096]{2,1,0:T(8,128)} %param.7) | copy-start | bytes 4718596
  40.9 268.8 %copy-start.1 = (f32[1,96,4096]{2,1,0:T(8,128)S(1)}, f32[1,96,4096]{2,1,0:T(8,128)}, u32[]{:S(2)}) copy-start(f32[1,96,4096]{2,1,0:T(8,128)} %param.8) | copy-start | bytes 4718596
  40.9 346.5 %all-gather.2.cloned.1.call-start = ((), (), s32[]{:S(2)}) async-start(), calls=%async_computation.3 | async-start | bytes 13369344 | tf_op jit(solution)/shard_map/all_gather | solution.py:34
Sparse Core Ops, SparseCore 0:
  41.0 268.6 reduce-scatter.1
  315.0 72.3 all-gather.1
where the time goes:
time: 746 us; the launch traced here: 743 us
  waiting for transfers between devices  341 us (46%)
  blocking collectives  147 us (20%)
  local copies, waits for them, and re-layouts  121 us (16%)
  other arithmetic  86.4 us (12%)
  matrix products  33.7 us (5%)
  between operations  14 us (2%)
    reduce_scatter x1, waiting for transfers between devices, local(): lax.psum_scatter(lax.dot_general(logit_grads, hidden_states, (((0,), (0,)...  269 us
    all_to_all x1, blocking collectives, local(): lax.all_to_all(copies, 'vocab', split_axis=2, concat_axis=0, tiled=True)  147 us
    unnamed x1, other arithmetic  81.3 us
    all_gather x1, waiting for transfers between devices, local(): copies = lax.all_gather(rounded, 'dp', axis=1, tiled=True)  72.5 us
    all_gather x1, local copies, waits for them, and re-layouts, local(): copies = lax.all_gather(rounded, 'dp', axis=1, tiled=True)  54.8 us
    unnamed x8, local copies, waits for them, and re-layouts  49.4 us
    dot_general x1, matrix products, local(): lax.dot_general(logit_grads, hidden_states, (((0,), (0,)), ((), ())), pre...  33.7 us
    all_to_all x1, local copies, waits for them, and re-layouts, local(): lax.all_to_all(copies, 'vocab', split_axis=2, concat_axis=0, tiled=True)  16.6 us
  transfers between devices with their start and end apart: 2, of which 2 were waited for; matrix products, arithmetic and copies ran while one was open for 0% of the time, Pallas kernels for 0%

commit v1 on v0

v1 whole, which is shorter than its diff:
```python
import jax
import jax.numpy as jnp
import numpy as np
from jax import lax
from jax.experimental import pallas as pl
from jax.experimental.pallas import tpu as pltpu
from jax.sharding import Mesh, PartitionSpec as P

STEP = 100

beta_one = 0.9
beta_two = 0.999
learn_rate = 0.001
decay_rate = 0.1
epsilon = 1e-08

F16 = jnp.float16
F32 = jnp.float32
BF16 = jnp.bfloat16
PARAMS = pltpu.CompilerParams(vmem_limit_bytes=48 * 2**20)

SWAP = [(0, 1), (1, 0)]
UP = [(i, (i + 1) % 4) for i in range(4)]
DOWN = [(i, (i + 3) % 4) for i in range(4)]

ROWS = 48
COLS = 256


def order_kernel(slot, grads, out):
    turned = grads[...].T
    for q in range(8):
        at = pl.multiple_of(slot[pl.program_id(0) * 8 + q] * 16, 16)
        out[pl.ds(at, 16), :] = turned[16 * q : 16 * q + 16]


def order_rows(slot, logit_grads):
    return pl.pallas_call(
        order_kernel,
        grid_spec=pltpu.PrefetchScalarGridSpec(
            num_scalar_prefetch=1,
            grid=(12,),
            in_specs=[pl.BlockSpec((2048, 128), lambda i, s: (0, i))],
            out_specs=pl.BlockSpec((1536, 2048), lambda i, s: (0, 0)),
        ),
        out_shape=jax.ShapeDtypeStruct((1536, 2048), BF16),
        compiler_params=PARAMS,
        name="order_rows",
    )(slot, logit_grads)


def product_kernel(rows, hidden, out):
    out[...] = jnp.dot(rows[...], hidden[...], preferred_element_type=F32)


def product(rows, hidden, part, half):
    return pl.pallas_call(
        product_kernel,
        grid=(8,),
        in_specs=[
            pl.BlockSpec((384, 2048), lambda w: (part, 0)),
            pl.BlockSpec((2048, COLS), lambda w: (0, 2 * w + half)),
        ],
        out_specs=pl.BlockSpec((384, COLS), lambda w: (0, w)),
        out_shape=jax.ShapeDtypeStruct((384, 8 * COLS), F32),
        compiler_params=PARAMS,
        cost_estimate=pl.CostEstimate(
            flops=2 * 384 * 2048 * 8 * COLS, bytes_accessed=13 * 2**20, transcendentals=0
        ),
        name=f"product_{part}_{half}",
    )(rows, hidden)


def adam_kernel(first_chunk, gradient, master, one, two, *rest):
    new_master, new_one, new_two, rounded = rest if first_chunk else rest[3:]
    g = gradient[...]
    m = beta_one * one[...] + (1.0 - beta_one) * g
    v = beta_two * two[...] + (1.0 - beta_two) * g * g
    first_hat = m / (1.0 - beta_one**STEP)
    second_hat = v / (1.0 - beta_two**STEP)
    old = master[...]
    new = old - learn_rate * (first_hat / (jnp.sqrt(second_hat) + epsilon) + decay_rate * old)
    new_master[...] = new
    new_one[...] = m
    new_two[...] = v
    rounded[...] = new.astype(BF16)[None]


def adam(gradient, state, outs, part, half):
    tile = pl.BlockSpec((ROWS, COLS), lambda w: (part, 2 * w + half))
    whole = pl.BlockSpec(memory_space=pl.ANY)
    given = () if outs is None else outs
    got = pl.pallas_call(
        lambda *refs: adam_kernel(outs is None, *refs),
        grid=(8,),
        in_specs=[pl.BlockSpec((ROWS, COLS), lambda w: (0, w)), tile, tile, tile] + [whole] * len(given),
        out_specs=[tile] * 3 + [pl.BlockSpec((1, ROWS, COLS), lambda w: (w, 0, 0))],
        out_shape=[jax.ShapeDtypeStruct((96, 4096), F32)] * 3 + [jax.ShapeDtypeStruct((8, ROWS, COLS), BF16)],
        input_output_aliases={} if outs is None else {4: 0, 5: 1, 6: 2},
        compiler_params=PARAMS,
        name=f"adam_{part}_{half}",
    )(gradient, *state, *given)
    return got[:3], got[3]


def place_kernel(first_chunk, dp, own, other, *rest):
    out = rest[-1]

    @pl.when(pl.program_id(0) == 0)
    def _():
        out[...] = own[...].reshape(out.shape)

    @pl.when(pl.program_id(0) == 1)
    def _():
        out[...] = other[...].reshape(out.shape)


def place(dp, own, other, head, part, half):
    given = () if head is None else (head,)
    return pl.pallas_call(
        lambda *refs: place_kernel(head is None, *refs),
        grid_spec=pltpu.PrefetchScalarGridSpec(
            num_scalar_prefetch=1,
            grid=(2, 8),
            in_specs=[
                pl.BlockSpec((1, 8, ROWS, COLS), lambda c, i, s: (jnp.where(c == 0, i, 7), 0, 0, 0)),
                pl.BlockSpec((1, 8, ROWS, COLS), lambda c, i, s: (jnp.where(c == 0, 0, i), 0, 0, 0)),
            ]
            + [pl.BlockSpec(memory_space=pl.ANY)] * len(given),
            out_specs=pl.BlockSpec((8, 1, ROWS, COLS), lambda c, i, s: (0, s[c * 8 + i], part, half)),
        ),
        out_shape=jax.ShapeDtypeStruct((8, 16, 96, 512), BF16),
        input_output_aliases={} if head is None else {3: 0},
        compiler_params=PARAMS,
        name=f"place_{part}_{half}",
    )(dp, own.reshape(8, 8, ROWS, COLS), other.reshape(8, 8, ROWS, COLS), *given)


def wide(a):
    return a.astype(F32)


def ring_sum(parts):
    to_up = lax.ppermute(parts(2, 0).astype(F16), "x", UP)
    to_down = lax.ppermute(parts(2, 1).astype(F16), "x", DOWN)
    up = jnp.concatenate([parts(1, 0) + wide(to_up), parts(1, 1)], 0).astype(F16)
    down = jnp.concatenate([parts(3, 0), parts(3, 1) + wide(to_down)], 0).astype(F16)
    from_down = lax.ppermute(up, "x", UP)
    from_up = lax.ppermute(down, "x", DOWN)
    own = jnp.concatenate([parts(0, 0), parts(0, 1)], 0)
    return own + wide(from_down) + wide(from_up)


def ring_gather(own):
    n = own.shape[0] // 2
    below = lax.ppermute(own, "x", UP)
    above = lax.ppermute(own, "x", DOWN)
    far_low = lax.ppermute(below[:n], "x", UP)
    far_high = lax.ppermute(above[n:], "x", DOWN)
    return jnp.stack([own, above, jnp.concatenate([far_low, far_high], 0), below])


def local(hidden_states, logit_grads, master, moment_one, moment_two):
    x, z, c = lax.axis_index("x"), lax.axis_index("zl"), lax.axis_index("c")
    dp = jnp.arange(16)
    ahead = (dp // 4 - x) % 4
    mine_z = (dp // 2 % 2 == z).astype(jnp.int32)
    mine_c = (dp % 2 == c).astype(jnp.int32)
    group = jnp.arange(96)
    slot = (((group % 6 // 3) * 2 + mine_c[group // 6]) * 8 + ahead[group // 6] * 2 + mine_z[group // 6]) * 3 + group % 3
    rel = jnp.arange(16)
    place_dp = ((x + rel % 4) % 4) * 4 + (z + rel // 4 % 2) % 2 * 2 + (c + rel // 8) % 2
    slot, place_dp = slot.astype(jnp.int32), place_dp.astype(jnp.int32)

    rows = order_rows(slot, logit_grads)
    state = (master[0], moment_one[0], moment_two[0])
    outs, head = None, None
    for half in range(2):
        for part in range(2):
            send = product(rows, hidden_states, 2 * part, half)
            keep = product(rows, hidden_states, 2 * part + 1, half)
            came = lax.ppermute(send, "c", SWAP)
            keep = keep.reshape(4, 2, ROWS, 8 * COLS)
            came = came.reshape(4, 2, ROWS, 8 * COLS)
            if part == 0:
                over = lax.ppermute((keep[:, 0] + came[:, 0]).astype(F16), "zl", SWAP)
                r = ROWS // 2
                terms = lambda k, a: (
                    keep[k, 1, a * r : a * r + r] + came[k, 1, a * r : a * r + r] + wide(over[k, a * r : a * r + r])
                )
                gradient = ring_sum(terms)
            else:
                terms = lambda k, a: keep[k, a] + came[k, a]
                total = ring_sum(terms).reshape(2, ROWS, 8 * COLS)
                over = lax.ppermute(total[0].astype(F16), "zl", SWAP)
                gradient = total[1] + wide(over)
            outs, rounded = adam(gradient, state, outs, part, half)
            mine = lax.all_to_all(rounded, ("y", "zh"), split_axis=0, concat_axis=0, tiled=True)
            if part == 0:
                row = ring_gather(mine)
                both = jnp.stack([row, lax.ppermute(row, "zl", SWAP)])
            else:
                pair = jnp.concatenate([mine, lax.ppermute(mine, "zl", SWAP)], 0)
                both = jnp.swapaxes(ring_gather(pair).reshape(4, 2, 8, ROWS, COLS), 0, 1)
            other = lax.ppermute(both, "c", SWAP)
            head = place(place_dp, both, other, head, part, half)
    return (*(o[None] for o in outs), head.reshape(12288, 512))


def solution(mesh):
    parts = Mesh(mesh.devices.reshape(4, 2, 2, 4, 2), ("x", "zl", "c", "y", "zh"))
    dp, vocab = ("x", "zl", "c"), ("y", "zh")
    held = P(vocab, dp, None)
    return jax.shard_map(
        local,
        mesh=parts,
        in_specs=(P(dp, None), P(dp, vocab), held, held, held),
        out_specs=(held, held, held, P(None, vocab)),
        check_vma=False,
    )
```

time: 746 us -> 329 us (0.44)
  waiting for transfers between devices: 341 us -> 50.8 us
  blocking collectives: 147 us -> 0 us
  Pallas kernels: 0 us -> 121 us
  local copies, waits for them, and re-layouts: 121 us -> 6.96 us
  starting transfers between devices: 0.26 us -> 92.6 us
  matrix products: 33.7 us -> 0 us
  other arithmetic: 86.4 us -> 53.9 us
  between operations: 14 us -> 1.21 us
    reduce_scatter x1 -> x0, waiting for transfers between devices: 269 us -> none  [local(): lax.psum_scatter(lax.dot_general(logit_grads, hidden_states, (((0,), (0,)...]
    all_to_all x1 -> x0, blocking collectives: 147 us -> none  [local(): lax.all_to_all(copies, 'vocab', split_axis=2, concat_axis=0, tiled=True)]
    pallas_call x0 -> x17, Pallas kernels: none -> 121 us  [the longest x8 72.9 us: product(): pl.pallas_call(product_kernel, grid=(8,), in_specs=[pl.BlockSpec((384, 20...]
    unnamed x1 -> x0, other arithmetic: 81.3 us -> none
    all_gather x1 -> x0, waiting for transfers between devices: 72.5 us -> none  [local(): copies = lax.all_gather(rounded, 'dp', axis=1, tiled=True)]
    ppermute x0 -> x48, starting transfers between devices: none -> 72 us  [the longest x4 25.7 us: local(): other = lax.ppermute(both, 'c', SWAP)]
    all_gather x1 -> x0, local copies, waits for them, and re-layouts: 54.8 us -> none  [local(): copies = lax.all_gather(rounded, 'dp', axis=1, tiled=True)]
    unnamed x8 -> x14, local copies, waits for them, and re-layouts: 49.4 us -> 3.78 us
  transfers between devices with their start and end apart: 2 -> 52, of which waited for: 2 -> 17; matrix products, arithmetic and copies ran while one was open for 0% -> 8% of each run, Pallas kernels for 0% -> 29%
where the time goes in v1:
time: 329 us; the launch traced here: 326 us
  Pallas kernels  121 us (37%)
  starting transfers between devices  92.6 us (28%)
  other arithmetic  53.9 us (16%)
  waiting for transfers between devices  50.8 us (15%)
  local copies, waits for them, and re-layouts  6.96 us (2%)
    pallas_call x8, Pallas kernels, product(): pl.pallas_call(product_kernel, grid=(8,), in_specs=[pl.BlockSpec((384, 20...  72.9 us
    add x1, other arithmetic, local(): ((group % 6 // 3 * 2 + mine_c[group // 6]) * 8 + ahead[group // 6] * 2 +...  30.1 us
    ppermute x4, starting transfers between devices, local(): other = lax.ppermute(both, 'c', SWAP)  25.7 us
    pallas_call x4, Pallas kernels, place(): pl.pallas_call(lambda *refs: place_kernel(head is None, *refs), grid_spec...  24.8 us
    all_to_all x4, starting transfers between devices, local(): lax.all_to_all(rounded, ('y', 'zh'), split_axis=0, concat_axis=0, tiled=T...  20.6 us
    pallas_call x4, Pallas kernels, adam(): pl.pallas_call(lambda *refs: adam_kernel(outs is None, *refs), grid=(8,),...  11.9 us
    pallas_call x1, Pallas kernels, order_rows(): pl.pallas_call(order_kernel, grid_spec=pltpu.PrefetchScalarGridSpec(num_s...  11.2 us
    ppermute x4, starting transfers between devices, ring_gather(): above = lax.ppermute(own, 'x', DOWN)  10.6 us
  transfers between devices with their start and end apart: 52, of which 17 were waited for; matrix products, arithmetic and copies ran while one was open for 8% of the time, Pallas kernels for 29%

profile of v1, /device:TPU:1, one launch (start us, length us, event | category | flops | bytes accessed | tf_op | source)
XLA Modules:
  0.0 326.2 jit_solution(10505306361840686395)
XLA Ops:
  2.8 30.1 %fusion.88.slot = s32[96]{0:T(128)S(1)} fusion(s32[]{:T(128)} %bitcast.52, s32[]{:T(128)} %bitcast.35, s32[]{:T(128)} %bitcast.18, s32[]{:T(128)} %bitcast.53, s32[]{:T(128)} %bitcast.36, s32[]{:T(128)} %bitcast.19, s32[]{:T(128)} %bitcast.54, s32[]{:T(128)} %bitcast.37, s32[]{:T(128)} %bitcast.20, s32[]{:T(128)} %bitcast.55, s32[]{:T(128)} %bitcast.38, ...), kind=kLoop, calls=%fused_computation.233 | loop fusion | flops 9504 | bytes 576 | tf_op jit(solution)/shard_map/add | solution.py:170
  32.9 11.2 %order_rows.1.rows = bf16[1536,2048]{1,0:T(8,128)(2,1)} custom-call(s32[96]{0:T(128)S(1)} %fusion.88.slot, bf16[2048,1536]{1,0:T(8,128)(2,1)} %grads.1), custom_call_target="tpu_custom_call" | custom-call | tf_op jit(solution)/shard_map/order_rows/pallas_call | solution.py:38
  44.1 9.8 %product_2_1.1 = f32[384,2048]{1,0:T(8,128)} custom-call(bf16[1536,2048]{1,0:T(8,128)(2,1)} %order_rows.1.rows, bf16[2048,4096]{1,0:T(8,128)(2,1)} %hidden.15), custom_call_target="tpu_custom_call" | custom-call | flops 3221225472 | bytes 13631488 | tf_op jit(solution)/shard_map/product_2_1/pallas_call | solution.py:57
  55.3 9.8 %product_0_1.1 = f32[384,2048]{1,0:T(8,128)} custom-call(bf16[1536,2048]{1,0:T(8,128)(2,1)} %order_rows.1.rows, bf16[2048,4096]{1,0:T(8,128)(2,1)} %hidden.15), custom_call_target="tpu_custom_call" | custom-call | flops 3221225472 | bytes 13631488 | tf_op jit(solution)/shard_map/product_0_1/pallas_call | solution.py:57
  65.1 9.8 %product_2_0.1 = f32[384,2048]{1,0:T(8,128)} custom-call(bf16[1536,2048]{1,0:T(8,128)(2,1)} %order_rows.1.rows, bf16[2048,4096]{1,0:T(8,128)(2,1)} %hidden.15), custom_call_target="tpu_custom_call" | custom-call | flops 3221225472 | bytes 13631488 | tf_op jit(solution)/shard_map/product_2_0/pallas_call | solution.py:57
  75.5 8.7 %product_0_0.1 = f32[384,2048]{1,0:T(8,128)S(1)} custom-call(bf16[1536,2048]{1,0:T(8,128)(2,1)} %order_rows.1.rows, bf16[2048,4096]{1,0:T(8,128)(2,1)} %hidden.15), custom_call_target="tpu_custom_call" | custom-call | flops 3221225472 | bytes 13631488 | tf_op jit(solution)/shard_map/product_0_0/pallas_call | solution.py:57
  84.3 8.7 %product_1_0.1 = f32[384,2048]{1,0:T(8,128)S(1)} custom-call(bf16[1536,2048]{1,0:T(8,128)(2,1)} %order_rows.1.rows, bf16[2048,4096]{1,0:T(8,128)(2,1)} %hidden.15), custom_call_target="tpu_custom_call" | custom-call | flops 3221225472 | bytes 13631488 | tf_op jit(solution)/shard_map/product_1_0/pallas_call | solution.py:57
  92.9 8.7 %product_3_0.1 = f32[384,2048]{1,0:T(8,128)S(1)} custom-call(bf16[1536,2048]{1,0:T(8,128)(2,1)} %order_rows.1.rows, bf16[2048,4096]{1,0:T(8,128)(2,1)} %hidden.15), custom_call_target="tpu_custom_call" | custom-call | flops 3221225472 | bytes 13631488 | tf_op jit(solution)/shard_map/product_3_0/pallas_call | solution.py:57
  101.6 8.7 %product_1_1.1 = f32[384,2048]{1,0:T(8,128)S(1)} custom-call(bf16[1536,2048]{1,0:T(8,128)(2,1)} %order_rows.1.rows, bf16[2048,4096]{1,0:T(8,128)(2,1)} %hidden.15), custom_call_target="tpu_custom_call" | custom-call | flops 3221225472 | bytes 13631488 | tf_op jit(solution)/shard_map/product_1_1/pallas_call | solution.py:57
  110.3 8.7 %product_3_1.1 = f32[384,2048]{1,0:T(8,128)S(1)} custom-call(bf16[1536,2048]{1,0:T(8,128)(2,1)} %order_rows.1.rows, bf16[2048,4096]{1,0:T(8,128)(2,1)} %hidden.15), custom_call_target="tpu_custom_call" | custom-call | flops 3221225472 | bytes 13631488 | tf_op jit(solution)/shard_map/product_3_1/pallas_call | solution.py:57
  119.0 2.0 fusion.32
  125.5 1.8 collective-permute-start.7
  127.3 2.0 fusion.36
  129.4 2.7 collective-permute-start.15
  139.9 4.2 %collective-permute-done.4 = f16[96,2048]{1,0:T(8,128)(2,1)S(1)} collective-permute-done((f16[96,2048]{1,0:T(8,128)(2,1)S(1)}, f16[96,2048]{1,0:T(8,128)(2,1)S(1)}, u32[]{:S(2)}, u32[]{:S(2)}) %collective-permute-start.4) | collective-permute-done | bytes 393248 | tf_op jit(solution)/shard_map/ppermute | solution.py:149
  147.3 5.1 %collective-permute-done.16 = f16[96,2048]{1,0:T(8,128)(2,1)S(1)} collective-permute-done((f16[96,2048]{1,0:T(8,128)(2,1)S(1)}, f16[96,2048]{1,0:T(8,128)(2,1)S(1)}, u32[]{:S(2)}, u32[]{:S(2)}) %collective-permute-start.16) | collective-permute-done | bytes 393248 | tf_op jit(solution)/shard_map/ppermute | solution.py:149
  155.2 5.7 %collective-permute-done.19 = f16[4,48,2048]{2,1,0:T(8,128)(2,1)S(1)} collective-permute-done((f16[4,48,2048]{2,1,0:T(8,128)(2,1)S(1)}, f16[4,48,2048]{2,1,0:T(8,128)(2,1)S(1)}, u32[]{:S(2)}, u32[]{:S(2)}) %collective-permute-start.19) | collective-permute-done | bytes 786464 | tf_op jit(solution)/shard_map/ppermute | solution.py:186
  162.0 7.4 %collective-permute-done.17 = f16[48,2048]{1,0:T(8,128)(2,1)S(1)} collective-permute-done((f16[48,2048]{1,0:T(8,128)(2,1)S(1)}, f16[48,2048]{1,0:T(8,128)(2,1)S(1)}, u32[]{:S(2)}, u32[]{:S(2)}) %collective-permute-start.17) | collective-permute-done | bytes 196640 | tf_op jit(solution)/shard_map/ppermute | solution.py:195
  173.4 1.7 fusion.59
  175.1 2.5 collective-permute-start.22
  180.2 3.1 collective-permute-start.23
  186.1 3.0 adam_0_0.1
  189.1 3.0 adam_1_0.1
  192.1 7.1 %all-to-all-start.2 = ((bf16[8,48,256]{2,1,0:T(8,128)(2,1)}), bf16[8,48,256]{2,1,0:T(8,128)(2,1)}, u32[]{:S(2)}, u32[]{:S(2)}) async-start(bf16[8,48,256]{2,1,0:T(8,128)(2,1)} %get-tuple-element.34), calls=%async_computation.2 | async-start | bytes 393216 | tf_op jit(solution)/shard_map/all_to_all | solution.py:198
  201.7 3.0 adam_0_1.1
  206.3 5.0 %all-to-all-start.1 = ((bf16[8,48,256]{2,1,0:T(8,128)(2,1)}), bf16[8,48,256]{2,1,0:T(8,128)(2,1)S(1)}, u32[]{:S(2)}, u32[]{:S(2)}) async-start(bf16[8,48,256]{2,1,0:T(8,128)(2,1)} %get-tuple-element.33), calls=%async_computation.1 | async-start | bytes 393216 | tf_op jit(solution)/shard_map/all_to_all | solution.py:198
  212.1 6.4 %all-to-all-done.1 = bf16[8,48,256]{2,1,0:T(8,128)(2,1)S(1)} async-done(((bf16[8,48,256]{2,1,0:T(8,128)(2,1)}), bf16[8,48,256]{2,1,0:T(8,128)(2,1)S(1)}, u32[]{:S(2)}, u32[]{:S(2)}) %all-to-all-start.1) | async-done | bytes 196640 | tf_op jit(solution)/shard_map/all_to_all | solution.py:198
  218.5 3.4 %all-to-all-start.3 = ((bf16[8,48,256]{2,1,0:T(8,128)(2,1)}), bf16[8,48,256]{2,1,0:T(8,128)(2,1)S(1)}, u32[]{:S(2)}, u32[]{:S(2)}) async-start(bf16[8,48,256]{2,1,0:T(8,128)(2,1)} %get-tuple-element.35), calls=%async_computation.3 | async-start | bytes 393216 | tf_op jit(solution)/shard_map/all_to_all | solution.py:198
  224.4 3.0 adam_1_1.1
  228.8 5.1 %all-to-all-start = ((bf16[8,48,256]{2,1,0:T(8,128)(2,1)}), bf16[8,48,256]{2,1,0:T(8,128)(2,1)S(1)}, u32[]{:S(2)}, u32[]{:S(2)}) async-start(bf16[8,48,256]{2,1,0:T(8,128)(2,1)} %get-tuple-element.32), calls=%async_computation | async-start | bytes 393216 | tf_op jit(solution)/shard_map/all_to_all | solution.py:198
  234.5 2.6 collective-permute-start.42
  237.1 2.7 collective-permute-start.30
  243.3 2.6 collective-permute-start.37
  247.0 2.4 collective-permute-start.33
  249.4 7.3 %collective-permute-done.32 = bf16[4,48,256]{2,1,0:T(8,128)(2,1)S(1)} collective-permute-done((bf16[4,48,256]{2,1,0:T(8,128)(2,1)S(1)}, bf16[4,48,256]{2,1,0:T(8,128)(2,1)S(1)}, u32[]{:S(2)}, u32[]{:S(2)}) %collective-permute-start.32) | collective-permute-done | bytes 98336 | tf_op jit(solution)/shard_map/ppermute | solution.py:158
  256.7 1.7 collective-permute-start.45
  258.6 2.7 collective-permute-start.25
  263.4 3.3 %collective-permute-done.26 = bf16[16,48,256]{2,1,0:T(8,128)(2,1)S(1)} collective-permute-done((bf16[16,48,256]{2,1,0:T(8,128)(2,1)S(1)}, bf16[16,48,256]{2,1,0:T(8,128)(2,1)S(1)}, u32[]{:S(2)}, u32[]{:S(2)}) %collective-permute-start.26) | collective-permute-done | bytes 393248 | tf_op jit(solution)/shard_map/ppermute | solution.py:156
  266.7 1.7 collective-permute-start.40
  269.6 1.7 collective-permute-start.28
  272.4 12.8 %collective-permute-start.41 = (bf16[2,4,8,48,256]{4,3,2,1,0:T(8,128)(2,1)S(1)}, bf16[2,4,8,48,256]{4,3,2,1,0:T(8,128)(2,1)S(1)}, u32[]{:S(2)}, u32[]{:S(2)}) collective-permute-start(bf16[2,4,8,48,256]{4,3,2,1,0:T(8,128)(2,1)S(1)} %get-tuple-element.64), channel_id=1, source_target_pairs={{0,8},{8,0},{1,9},{9,1},{2,10},{10,2},{3,11},{11,3},{4,12},{12,4},... | collective-permute-start | bytes 4718600 | tf_op jit(solution)/shard_map/ppermute | solution.py:205
  285.4 4.5 %collective-permute-start.35 = (bf16[2,4,8,48,256]{4,3,2,1,0:T(8,128)(2,1)S(1)}, bf16[2,4,8,48,256]{4,3,2,1,0:T(8,128)(2,1)S(1)}, u32[]{:S(2)}, u32[]{:S(2)}) collective-permute-start(bf16[2,4,8,48,256]{4,3,2,1,0:T(8,128)(2,1)S(1)} %pad_maximum_fusion.1), channel_id=1, source_target_pairs={{0,8},{8,0},{1,9},{9,1},{2,10},{10,2},{3,11},{11,3},{4,12},{12,4},... | collective-permute-start | bytes 4718600 | tf_op jit(solution)/shard_map/ppermute | solution.py:205
  290.1 8.3 %collective-permute-start.47 = (bf16[2,4,8,48,256]{4,3,2,1,0:T(8,128)(2,1)S(1)}, bf16[2,4,8,48,256]{4,3,2,1,0:T(8,128)(2,1)S(1)}, u32[]{:S(2)}, u32[]{:S(2)}) collective-permute-start(bf16[2,4,8,48,256]{4,3,2,1,0:T(8,128)(2,1)S(1)} %pad_maximum_fusion.3), channel_id=1, source_target_pairs={{0,8},{8,0},{1,9},{9,1},{2,10},{10,2},{3,11},{11,3},{4,12},{12,4},... | collective-permute-start | bytes 4718600 | tf_op jit(solution)/shard_map/ppermute | solution.py:205
  298.8 2.7 collective-permute-done.47
  301.4 6.2 %place_0_0.1.refs_3_ = bf16[8,16,96,512]{3,2,1,0:T(8,128)(2,1)} custom-call(s32[16]{0:T(128)S(1)} %fusion.90.refs_0_, bf16[8,8,48,256]{3,2,1,0:T(8,128)(2,1)S(1)} %bitcast.523, bf16[8,8,48,256]{3,2,1,0:T(8,128)(2,1)S(1)} %bitcast.527), custom_call_target="tpu_custom_call" | custom-call | tf_op jit(solution)/shard_map/place_0_0/pallas_call | solution.py:120
  307.6 6.2 %place_1_0.1.refs_3_ = bf16[8,16,96,512]{3,2,1,0:T(8,128)(2,1)} custom-call(s32[16]{0:T(128)S(1)} %fusion.90.refs_0_, bf16[8,8,48,256]{3,2,1,0:T(8,128)(2,1)S(1)} %bitcast.525, bf16[8,8,48,256]{3,2,1,0:T(8,128)(2,1)S(1)} %bitcast.528, bf16[8,16,96,512]{3,2,1,0:T(8,128)(2,1)} %place_0_0.1.refs_3_), custom_call_target="tpu_custom_call", output_to_operand_aliasing={{}: (3, {})} | custom-call | tf_op jit(solution)/shard_map/place_1_0/pallas_call | solution.py:120
  313.8 6.2 %place_0_1.1.refs_3_ = bf16[8,16,96,512]{3,2,1,0:T(8,128)(2,1)} custom-call(s32[16]{0:T(128)S(1)} %fusion.90.refs_0_, bf16[8,8,48,256]{3,2,1,0:T(8,128)(2,1)S(1)} %bitcast.524, bf16[8,8,48,256]{3,2,1,0:T(8,128)(2,1)S(1)} %bitcast.529, bf16[8,16,96,512]{3,2,1,0:T(8,128)(2,1)} %place_1_0.1.refs_3_), custom_call_target="tpu_custom_call", output_to_operand_aliasing={{}: (3, {})} | custom-call | tf_op jit(solution)/shard_map/place_0_1/pallas_call | solution.py:120
  320.0 6.2 %place_1_1.1 = bf16[8,16,96,512]{3,2,1,0:T(8,128)(2,1)} custom-call(s32[16]{0:T(128)S(1)} %fusion.90.refs_0_, bf16[8,8,48,256]{3,2,1,0:T(8,128)(2,1)S(1)} %bitcast.526, bf16[8,8,48,256]{3,2,1,0:T(8,128)(2,1)S(1)} %bitcast.530, bf16[8,16,96,512]{3,2,1,0:T(8,128)(2,1)} %place_0_1.1.refs_3_), custom_call_target="tpu_custom_call", output_to_operand_aliasing={{}: (3, {})} | custom-call | tf_op jit(solution)/shard_map/place_1_1/pallas_call | solution.py:120
  (143 shorter events, 52.0 us)
Async XLA Ops:
  53.9 65.1 %collective-permute-start = (f32[384,2048]{1,0:T(8,128)}, f32[384,2048]{1,0:T(8,128)}, u32[]{:S(2)}, u32[]{:S(2)}) collective-permute-start(f32[384,2048]{1,0:T(8,128)} %product_2_1.1), channel_id=1, source_target_pairs={{0,8},{8,0},{1,9},{9,1},{2,10},{10,2},{3,11},{11,3},{4,12},{12,4},... | collective-permute-start | bytes 9437192 | tf_op jit(solution)/shard_map/ppermute | solution.py:182
  65.1 58.7 %collective-permute-start.6 = (f32[384,2048]{1,0:T(8,128)}, f32[384,2048]{1,0:T(8,128)}, u32[]{:S(2)}, u32[]{:S(2)}) collective-permute-start(f32[384,2048]{1,0:T(8,128)} %product_0_1.1), channel_id=1, source_target_pairs={{0,8},{8,0},{1,9},{9,1},{2,10},{10,2},{3,11},{11,3},{4,12},{12,4},... | collective-permute-start | bytes 9437192 | tf_op jit(solution)/shard_map/ppermute | solution.py:182
  75.0 52.3 %collective-permute-start.12 = (f32[384,2048]{1,0:T(8,128)}, f32[384,2048]{1,0:T(8,128)}, u32[]{:S(2)}, u32[]{:S(2)}) collective-permute-start(f32[384,2048]{1,0:T(8,128)} %product_2_0.1), channel_id=1, source_target_pairs={{0,8},{8,0},{1,9},{9,1},{2,10},{10,2},{3,11},{11,3},{4,12},{12,4},... | collective-permute-start | bytes 9437192 | tf_op jit(solution)/shard_map/ppermute | solution.py:182
  84.2 45.2 %collective-permute-start.18 = (f32[384,2048]{1,0:T(8,128)S(1)}, f32[384,2048]{1,0:T(8,128)}, u32[]{:S(2)}, u32[]{:S(2)}) collective-permute-start(f32[384,2048]{1,0:T(8,128)S(1)} %product_0_0.1), channel_id=1, source_target_pairs={{0,8},{8,0},{1,9},{9,1},{2,10},{10,2},{3,11},{11,3},{4,12},{12,4},... | collective-permute-start | bytes 9437192 | tf_op jit(solution)/shard_map/ppermute | solution.py:182
  121.0 12.6 %collective-permute-start.1 = (f16[48,2048]{1,0:T(8,128)(2,1)S(1)}, f16[48,2048]{1,0:T(8,128)(2,1)S(1)}, u32[]{:S(2)}, u32[]{:S(2)}) collective-permute-start(f16[48,2048]{1,0:T(8,128)(2,1)S(1)} %get-tuple-element.58), channel_id=1, source_target_pairs={{0,32},{32,64},{64,96},{96,0},{1,33},{33,65},{65,97},{97,1},{2,34}... | collective-permute-start | bytes 589832 | tf_op jit(solution)/shard_map/ppermute | solution.py:144
  122.4 11.4 %collective-permute-start.3 = (f16[48,2048]{1,0:T(8,128)(2,1)S(1)}, f16[48,2048]{1,0:T(8,128)(2,1)S(1)}, u32[]{:S(2)}, u32[]{:S(2)}) collective-permute-start(f16[48,2048]{1,0:T(8,128)(2,1)S(1)} %get-tuple-element.59), channel_id=1, source_target_pairs={{0,96},{32,0},{64,32},{96,64},{1,97},{33,1},{65,33},{97,65},{2,98}... | collective-permute-start | bytes 589832 | tf_op jit(solution)/shard_map/ppermute | solution.py:145
  125.5 28.6 %collective-permute-start.7 = (f16[4,48,2048]{2,1,0:T(8,128)(2,1)S(1)}, f16[4,48,2048]{2,1,0:T(8,128)(2,1)S(1)}, u32[]{:S(2)}, u32[]{:S(2)}) collective-permute-start(f16[4,48,2048]{2,1,0:T(8,128)(2,1)S(1)} %fusion.2), channel_id=1, source_target_pairs={{0,16},{16,0},{1,17},{17,1},{2,18},{18,2},{3,19},{19,3},{4,20},{20... | collective-permute-start | bytes 2359304 | tf_op jit(solution)/shard_map/ppermute | solution.py:186
  129.3 6.4 %collective-permute-start.13 = (f16[48,2048]{1,0:T(8,128)(2,1)S(1)}, f16[48,2048]{1,0:T(8,128)(2,1)S(1)}, u32[]{:S(2)}, u32[]{:S(2)}) collective-permute-start(f16[48,2048]{1,0:T(8,128)(2,1)S(1)} %get-tuple-element.50), channel_id=1, source_target_pairs={{0,32},{32,64},{64,96},{96,0},{1,33},{33,65},{65,97},{97,1},{2,34}... | collective-permute-start | bytes 589832 | tf_op jit(solution)/shard_map/ppermute | solution.py:144
  129.4 7.6 %collective-permute-start.15 = (f16[48,2048]{1,0:T(8,128)(2,1)S(1)}, f16[48,2048]{1,0:T(8,128)(2,1)S(1)}, u32[]{:S(2)}, u32[]{:S(2)}) collective-permute-start(f16[48,2048]{1,0:T(8,128)(2,1)S(1)} %get-tuple-element.51), channel_id=1, source_target_pairs={{0,96},{32,0},{64,32},{96,64},{1,97},{33,1},{65,33},{97,65},{2,98}... | collective-permute-start | bytes 589832 | tf_op jit(solution)/shard_map/ppermute | solution.py:145
  133.7 27.2 %collective-permute-start.19 = (f16[4,48,2048]{2,1,0:T(8,128)(2,1)S(1)}, f16[4,48,2048]{2,1,0:T(8,128)(2,1)S(1)}, u32[]{:S(2)}, u32[]{:S(2)}) collective-permute-start(f16[4,48,2048]{2,1,0:T(8,128)(2,1)S(1)} %fusion.3), channel_id=1, source_target_pairs={{0,16},{16,0},{1,17},{17,1},{2,18},{18,2},{3,19},{19,3},{4,20},{20... | collective-permute-start | bytes 2359304 | tf_op jit(solution)/shard_map/ppermute | solution.py:186
  135.2 8.8 %collective-permute-start.4 = (f16[96,2048]{1,0:T(8,128)(2,1)S(1)}, f16[96,2048]{1,0:T(8,128)(2,1)S(1)}, u32[]{:S(2)}, u32[]{:S(2)}) collective-permute-start(f16[96,2048]{1,0:T(8,128)(2,1)S(1)} %pad_maximum_fusion.7), channel_id=1, source_target_pairs={{0,96},{32,0},{64,32},{96,64},{1,97},{33,1},{65,33},{97,65},{2,98}... | collective-permute-start | bytes 1179656 | tf_op jit(solution)/shard_map/ppermute | solution.py:149
  135.6 9.6 %collective-permute-start.2 = (f16[96,2048]{1,0:T(8,128)(2,1)S(1)}, f16[96,2048]{1,0:T(8,128)(2,1)S(1)}, u32[]{:S(2)}, u32[]{:S(2)}) collective-permute-start(f16[96,2048]{1,0:T(8,128)(2,1)S(1)} %pad_maximum_fusion.6), channel_id=1, source_target_pairs={{0,32},{32,64},{64,96},{96,0},{1,33},{33,65},{65,97},{97,1},{2,34}... | collective-permute-start | bytes 1179656 | tf_op jit(solution)/shard_map/ppermute | solution.py:148
  138.3 14.1 %collective-permute-start.16 = (f16[96,2048]{1,0:T(8,128)(2,1)S(1)}, f16[96,2048]{1,0:T(8,128)(2,1)S(1)}, u32[]{:S(2)}, u32[]{:S(2)}) collective-permute-start(f16[96,2048]{1,0:T(8,128)(2,1)S(1)} %pad_maximum_fusion.9), channel_id=1, source_target_pairs={{0,96},{32,0},{64,32},{96,64},{1,97},{33,1},{65,33},{97,65},{2,98}... | collective-permute-start | bytes 1179656 | tf_op jit(solution)/shard_map/ppermute | solution.py:149
  144.0 8.4 %collective-permute-start.14 = (f16[96,2048]{1,0:T(8,128)(2,1)S(1)}, f16[96,2048]{1,0:T(8,128)(2,1)S(1)}, u32[]{:S(2)}, u32[]{:S(2)}) collective-permute-start(f16[96,2048]{1,0:T(8,128)(2,1)S(1)} %pad_maximum_fusion.8), channel_id=1, source_target_pairs={{0,32},{32,64},{64,96},{96,0},{1,33},{33,65},{65,97},{97,1},{2,34}... | collective-permute-start | bytes 1179656 | tf_op jit(solution)/shard_map/ppermute | solution.py:148
  146.2 75.7 %collective-permute-start.5 = (f16[48,2048]{1,0:T(8,128)(2,1)}, f16[48,2048]{1,0:T(8,128)(2,1)}, u32[]{:S(2)}, u32[]{:S(2)}) collective-permute-start(f16[48,2048]{1,0:T(8,128)(2,1)} %slice_convert_fusion.1), channel_id=1, source_target_pairs={{0,16},{16,0},{1,17},{17,1},{2,18},{18,2},{3,19},{19,3},{4,20},{20... | collective-permute-start | bytes 589832 | tf_op jit(solution)/shard_map/ppermute | solution.py:195
  152.6 16.7 %collective-permute-start.17 = (f16[48,2048]{1,0:T(8,128)(2,1)S(1)}, f16[48,2048]{1,0:T(8,128)(2,1)S(1)}, u32[]{:S(2)}, u32[]{:S(2)}) collective-permute-start(f16[48,2048]{1,0:T(8,128)(2,1)S(1)} %slice_convert_fusion), channel_id=1, source_target_pairs={{0,16},{16,0},{1,17},{17,1},{2,18},{18,2},{3,19},{19,3},{4,20},{20... | collective-permute-start | bytes 589832 | tf_op jit(solution)/shard_map/ppermute | solution.py:195
  155.0 14.4 %collective-permute-start.8 = (f16[24,2048]{1,0:T(8,128)(2,1)S(1)}, f16[24,2048]{1,0:T(8,128)(2,1)S(1)}, u32[]{:S(2)}, u32[]{:S(2)}) collective-permute-start(f16[24,2048]{1,0:T(8,128)(2,1)S(1)} %fusion.79), channel_id=1, source_target_pairs={{0,32},{32,64},{64,96},{96,0},{1,33},{33,65},{65,97},{97,1},{2,34}... | collective-permute-start | bytes 294920 | tf_op jit(solution)/shard_map/ppermute | solution.py:144
  161.9 11.5 %collective-permute-start.20 = (f16[24,2048]{1,0:T(8,128)(2,1)S(1)}, f16[24,2048]{1,0:T(8,128)(2,1)S(1)}, u32[]{:S(2)}, u32[]{:S(2)}) collective-permute-start(f16[24,2048]{1,0:T(8,128)(2,1)S(1)} %fusion.55), channel_id=1, source_target_pairs={{0,32},{32,64},{64,96},{96,0},{1,33},{33,65},{65,97},{97,1},{2,34}... | collective-permute-start | bytes 294920 | tf_op jit(solution)/shard_map/ppermute | solution.py:144
  171.1 12.3 %collective-permute-start.10 = (f16[24,2048]{1,0:T(8,128)(2,1)S(1)}, f16[24,2048]{1,0:T(8,128)(2,1)S(1)}, u32[]{:S(2)}, u32[]{:S(2)}) collective-permute-start(f16[24,2048]{1,0:T(8,128)(2,1)S(1)} %get-tuple-element.43), channel_id=1, source_target_pairs={{0,96},{32,0},{64,32},{96,64},{1,97},{33,1},{65,33},{97,65},{2,98}... | collective-permute-start | bytes 294920 | tf_op jit(solution)/shard_map/ppermute | solution.py:145
  173.1 26.1 %collective-permute-start.9 = (f16[48,2048]{1,0:T(8,128)(2,1)}, f16[48,2048]{1,0:T(8,128)(2,1)}, u32[]{:S(2)}, u32[]{:S(2)}) collective-permute-start(f16[48,2048]{1,0:T(8,128)(2,1)} %pad_maximum_fusion.12), channel_id=1, source_target_pairs={{0,32},{32,64},{64,96},{96,0},{1,33},{33,65},{65,97},{97,1},{2,34}... | collective-permute-start | bytes 589832 | tf_op jit(solution)/shard_map/ppermute | solution.py:148
  177.6 7.5 %collective-permute-start.21 = (f16[48,2048]{1,0:T(8,128)(2,1)S(1)}, f16[48,2048]{1,0:T(8,128)(2,1)S(1)}, u32[]{:S(2)}, u32[]{:S(2)}) collective-permute-start(f16[48,2048]{1,0:T(8,128)(2,1)S(1)} %pad_maximum_fusion.14), channel_id=1, source_target_pairs={{0,32},{32,64},{64,96},{96,0},{1,33},{33,65},{65,97},{97,1},{2,34}... | collective-permute-start | bytes 589832 | tf_op jit(solution)/shard_map/ppermute | solution.py:148
  185.1 14.1 %collective-permute-start.11 = (f16[48,2048]{1,0:T(8,128)(2,1)}, f16[48,2048]{1,0:T(8,128)(2,1)}, u32[]{:S(2)}, u32[]{:S(2)}) collective-permute-start(f16[48,2048]{1,0:T(8,128)(2,1)} %pad_maximum_fusion.13), channel_id=1, source_target_pairs={{0,96},{32,0},{64,32},{96,64},{1,97},{33,1},{65,33},{97,65},{2,98}... | collective-permute-start | bytes 589832 | tf_op jit(solution)/shard_map/ppermute | solution.py:149
  192.1 14.3 %all-to-all-start.2 = ((bf16[8,48,256]{2,1,0:T(8,128)(2,1)}), bf16[8,48,256]{2,1,0:T(8,128)(2,1)}, u32[]{:S(2)}, u32[]{:S(2)}) async-start(bf16[8,48,256]{2,1,0:T(8,128)(2,1)} %get-tuple-element.34), calls=%async_computation.2 | async-start | bytes 393216 | tf_op jit(solution)/shard_map/all_to_all | solution.py:198
  206.3 12.2 %all-to-all-start.1 = ((bf16[8,48,256]{2,1,0:T(8,128)(2,1)}), bf16[8,48,256]{2,1,0:T(8,128)(2,1)S(1)}, u32[]{:S(2)}, u32[]{:S(2)}) async-start(bf16[8,48,256]{2,1,0:T(8,128)(2,1)} %get-tuple-element.33), calls=%async_computation.1 | async-start | bytes 393216 | tf_op jit(solution)/shard_map/all_to_all | solution.py:198
  211.3 29.6 %collective-permute-start.36 = (bf16[8,48,256]{2,1,0:T(8,128)(2,1)}, bf16[8,48,256]{2,1,0:T(8,128)(2,1)}, u32[]{:S(2)}, u32[]{:S(2)}) collective-permute-start(bf16[8,48,256]{2,1,0:T(8,128)(2,1)} %all-to-all-done.2), channel_id=1, source_target_pairs={{0,16},{16,0},{1,17},{17,1},{2,18},{18,2},{3,19},{19,3},{4,20},{20... | collective-permute-start | bytes 589832 | tf_op jit(solution)/shard_map/ppermute | solution.py:203
  218.5 10.4 %all-to-all-start.3 = ((bf16[8,48,256]{2,1,0:T(8,128)(2,1)}), bf16[8,48,256]{2,1,0:T(8,128)(2,1)S(1)}, u32[]{:S(2)}, u32[]{:S(2)}) async-start(bf16[8,48,256]{2,1,0:T(8,128)(2,1)} %get-tuple-element.35), calls=%async_computation.3 | async-start | bytes 393216 | tf_op jit(solution)/shard_map/all_to_all | solution.py:198
  228.8 12.1 %all-to-all-start = ((bf16[8,48,256]{2,1,0:T(8,128)(2,1)}), bf16[8,48,256]{2,1,0:T(8,128)(2,1)S(1)}, u32[]{:S(2)}, u32[]{:S(2)}) async-start(bf16[8,48,256]{2,1,0:T(8,128)(2,1)} %get-tuple-element.32), calls=%async_computation | async-start | bytes 393216 | tf_op jit(solution)/shard_map/all_to_all | solution.py:198
  233.9 8.7 %collective-permute-start.43 = (bf16[8,48,256]{2,1,0:T(8,128)(2,1)S(1)}, bf16[8,48,256]{2,1,0:T(8,128)(2,1)S(1)}, u32[]{:S(2)}, u32[]{:S(2)}) collective-permute-start(bf16[8,48,256]{2,1,0:T(8,128)(2,1)S(1)} %all-to-all-done.3), channel_id=1, source_target_pairs={{0,32},{32,64},{64,96},{96,0},{1,33},{33,65},{65,97},{97,1},{2,34}... | collective-permute-start | bytes 589832 | tf_op jit(solution)/shard_map/ppermute | solution.py:156
  234.5 8.8 %collective-permute-start.42 = (bf16[8,48,256]{2,1,0:T(8,128)(2,1)S(1)}, bf16[8,48,256]{2,1,0:T(8,128)(2,1)S(1)}, u32[]{:S(2)}, u32[]{:S(2)}) collective-permute-start(bf16[8,48,256]{2,1,0:T(8,128)(2,1)S(1)} %all-to-all-done.3), channel_id=1, source_target_pairs={{0,96},{32,0},{64,32},{96,64},{1,97},{33,1},{65,33},{97,65},{2,98}... | collective-permute-start | bytes 589832 | tf_op jit(solution)/shard_map/ppermute | solution.py:157
  237.1 8.8 %collective-permute-start.31 = (bf16[8,48,256]{2,1,0:T(8,128)(2,1)S(1)}, bf16[8,48,256]{2,1,0:T(8,128)(2,1)S(1)}, u32[]{:S(2)}, u32[]{:S(2)}) collective-permute-start(bf16[8,48,256]{2,1,0:T(8,128)(2,1)S(1)} %all-to-all-done.1), channel_id=1, source_target_pairs={{0,32},{32,64},{64,96},{96,0},{1,33},{33,65},{65,97},{97,1},{2,34}... | collective-permute-start | bytes 589832 | tf_op jit(solution)/shard_map/ppermute | solution.py:156
  237.1 8.9 %collective-permute-start.30 = (bf16[8,48,256]{2,1,0:T(8,128)(2,1)S(1)}, bf16[8,48,256]{2,1,0:T(8,128)(2,1)S(1)}, u32[]{:S(2)}, u32[]{:S(2)}) collective-permute-start(bf16[8,48,256]{2,1,0:T(8,128)(2,1)S(1)} %all-to-all-done.1), channel_id=1, source_target_pairs={{0,96},{32,0},{64,32},{96,64},{1,97},{33,1},{65,33},{97,65},{2,98}... | collective-permute-start | bytes 589832 | tf_op jit(solution)/shard_map/ppermute | solution.py:157
  241.0 6.0 %collective-permute-start.24 = (bf16[8,48,256]{2,1,0:T(8,128)(2,1)S(1)}, bf16[8,48,256]{2,1,0:T(8,128)(2,1)S(1)}, u32[]{:S(2)}, u32[]{:S(2)}) collective-permute-start(bf16[8,48,256]{2,1,0:T(8,128)(2,1)S(1)} %all-to-all-done), channel_id=1, source_target_pairs={{0,16},{16,0},{1,17},{17,1},{2,18},{18,2},{3,19},{19,3},{4,20},{20... | collective-permute-start | bytes 589832 | tf_op jit(solution)/shard_map/ppermute | solution.py:203
  242.7 19.6 %collective-permute-start.38 = (bf16[16,48,256]{2,1,0:T(8,128)(2,1)S(1)}, bf16[16,48,256]{2,1,0:T(8,128)(2,1)S(1)}, u32[]{:S(2)}, u32[]{:S(2)}) collective-permute-start(bf16[16,48,256]{2,1,0:T(8,128)(2,1)S(1)} %constant_dynamic-update-slice_fusion.2), channel_id=1, source_target_pairs={{0,32},{32,64},{64,96},{96,0},{1,33},{33,65},{65,97},{97,1},{2,34}... | collective-permute-start | bytes 1179656 | tf_op jit(solution)/shard_map/ppermute | solution.py:156
  243.3 19.7 %collective-permute-start.37 = (bf16[16,48,256]{2,1,0:T(8,128)(2,1)S(1)}, bf16[16,48,256]{2,1,0:T(8,128)(2,1)S(1)}, u32[]{:S(2)}, u32[]{:S(2)}) collective-permute-start(bf16[16,48,256]{2,1,0:T(8,128)(2,1)S(1)} %constant_dynamic-update-slice_fusion.2), channel_id=1, source_target_pairs={{0,96},{32,0},{64,32},{96,64},{1,97},{33,1},{65,33},{97,65},{2,98}... | collective-permute-start | bytes 1179656 | tf_op jit(solution)/shard_map/ppermute | solution.py:157
  246.0 12.6 %collective-permute-start.44 = (bf16[4,48,256]{2,1,0:T(8,128)(2,1)S(1)}, bf16[4,48,256]{2,1,0:T(8,128)(2,1)S(1)}, u32[]{:S(2)}, u32[]{:S(2)}) collective-permute-start(bf16[4,48,256]{2,1,0:T(8,128)(2,1)S(1)} %slice.535), channel_id=1, source_target_pairs={{0,32},{32,64},{64,96},{96,0},{1,33},{33,65},{65,97},{97,1},{2,34}... | collective-permute-start | bytes 294920 | tf_op jit(solution)/shard_map/ppermute | solution.py:158
  246.1 10.6 %collective-permute-start.32 = (bf16[4,48,256]{2,1,0:T(8,128)(2,1)S(1)}, bf16[4,48,256]{2,1,0:T(8,128)(2,1)S(1)}, u32[]{:S(2)}, u32[]{:S(2)}) collective-permute-start(bf16[4,48,256]{2,1,0:T(8,128)(2,1)S(1)} %slice.531), channel_id=1, source_target_pairs={{0,32},{32,64},{64,96},{96,0},{1,33},{33,65},{65,97},{97,1},{2,34}... | collective-permute-start | bytes 294920 | tf_op jit(solution)/shard_map/ppermute | solution.py:158
  247.0 11.4 %collective-permute-start.33 = (bf16[4,48,256]{2,1,0:T(8,128)(2,1)S(1)}, bf16[4,48,256]{2,1,0:T(8,128)(2,1)S(1)}, u32[]{:S(2)}, u32[]{:S(2)}) collective-permute-start(bf16[4,48,256]{2,1,0:T(8,128)(2,1)S(1)} %slice.532), channel_id=1, source_target_pairs={{0,96},{32,0},{64,32},{96,64},{1,97},{33,1},{65,33},{97,65},{2,98}... | collective-permute-start | bytes 294920 | tf_op jit(solution)/shard_map/ppermute | solution.py:159
  258.4 8.3 %collective-permute-start.26 = (bf16[16,48,256]{2,1,0:T(8,128)(2,1)S(1)}, bf16[16,48,256]{2,1,0:T(8,128)(2,1)S(1)}, u32[]{:S(2)}, u32[]{:S(2)}) collective-permute-start(bf16[16,48,256]{2,1,0:T(8,128)(2,1)S(1)} %constant_dynamic-update-slice_fusion), channel_id=1, source_target_pairs={{0,32},{32,64},{64,96},{96,0},{1,33},{33,65},{65,97},{97,1},{2,34}... | collective-permute-start | bytes 1179656 | tf_op jit(solution)/shard_map/ppermute | solution.py:156
  258.6 9.8 %collective-permute-start.25 = (bf16[16,48,256]{2,1,0:T(8,128)(2,1)S(1)}, bf16[16,48,256]{2,1,0:T(8,128)(2,1)S(1)}, u32[]{:S(2)}, u32[]{:S(2)}) collective-permute-start(bf16[16,48,256]{2,1,0:T(8,128)(2,1)S(1)} %constant_dynamic-update-slice_fusion), channel_id=1, source_target_pairs={{0,96},{32,0},{64,32},{96,64},{1,97},{33,1},{65,33},{97,65},{2,98}... | collective-permute-start | bytes 1179656 | tf_op jit(solution)/shard_map/ppermute | solution.py:157
  261.4 23.9 %collective-permute-start.34 = (bf16[4,8,48,256]{3,2,1,0:T(8,128)(2,1)S(1)}, bf16[4,8,48,256]{3,2,1,0:T(8,128)(2,1)S(1)}, u32[]{:S(2)}, u32[]{:S(2)}) collective-permute-start(bf16[4,8,48,256]{3,2,1,0:T(8,128)(2,1)S(1)} %get-tuple-element.71), channel_id=1, source_target_pairs={{0,16},{16,0},{1,17},{17,1},{2,18},{18,2},{3,19},{19,3},{4,20},{20... | collective-permute-start | bytes 2359304 | tf_op jit(solution)/shard_map/ppermute | solution.py:201
  262.3 27.7 %collective-permute-start.46 = (bf16[4,8,48,256]{3,2,1,0:T(8,128)(2,1)S(1)}, bf16[4,8,48,256]{3,2,1,0:T(8,128)(2,1)S(1)}, u32[]{:S(2)}, u32[]{:S(2)}) collective-permute-start(bf16[4,8,48,256]{3,2,1,0:T(8,128)(2,1)S(1)} %get-tuple-element.69), channel_id=1, source_target_pairs={{0,16},{16,0},{1,17},{17,1},{2,18},{18,2},{3,19},{19,3},{4,20},{20... | collective-permute-start | bytes 2359304 | tf_op jit(solution)/shard_map/ppermute | solution.py:201
  263.1 6.5 %collective-permute-start.39 = (bf16[8,48,256]{2,1,0:T(8,128)(2,1)S(1)}, bf16[8,48,256]{2,1,0:T(8,128)(2,1)S(1)}, u32[]{:S(2)}, u32[]{:S(2)}) collective-permute-start(bf16[8,48,256]{2,1,0:T(8,128)(2,1)S(1)} %slice.533), channel_id=1, source_target_pairs={{0,32},{32,64},{64,96},{96,0},{1,33},{33,65},{65,97},{97,1},{2,34}... | collective-permute-start | bytes 589832 | tf_op jit(solution)/shard_map/ppermute | solution.py:158
  268.5 16.8 %collective-permute-start.27 = (bf16[8,48,256]{2,1,0:T(8,128)(2,1)S(1)}, bf16[8,48,256]{2,1,0:T(8,128)(2,1)S(1)}, u32[]{:S(2)}, u32[]{:S(2)}) collective-permute-start(bf16[8,48,256]{2,1,0:T(8,128)(2,1)S(1)} %slice.529), channel_id=1, source_target_pairs={{0,32},{32,64},{64,96},{96,0},{1,33},{33,65},{65,97},{97,1},{2,34}... | collective-permute-start | bytes 589832 | tf_op jit(solution)/shard_map/ppermute | solution.py:158
  269.6 15.6 %collective-permute-start.28 = (bf16[8,48,256]{2,1,0:T(8,128)(2,1)S(1)}, bf16[8,48,256]{2,1,0:T(8,128)(2,1)S(1)}, u32[]{:S(2)}, u32[]{:S(2)}) collective-permute-start(bf16[8,48,256]{2,1,0:T(8,128)(2,1)S(1)} %slice.530), channel_id=1, source_target_pairs={{0,96},{32,0},{64,32},{96,64},{1,97},{33,1},{65,33},{97,65},{2,98}... | collective-permute-start | bytes 589832 | tf_op jit(solution)/shard_map/ppermute | solution.py:159
  272.4 35.2 %collective-permute-start.41 = (bf16[2,4,8,48,256]{4,3,2,1,0:T(8,128)(2,1)S(1)}, bf16[2,4,8,48,256]{4,3,2,1,0:T(8,128)(2,1)S(1)}, u32[]{:S(2)}, u32[]{:S(2)}) collective-permute-start(bf16[2,4,8,48,256]{4,3,2,1,0:T(8,128)(2,1)S(1)} %get-tuple-element.64), channel_id=1, source_target_pairs={{0,8},{8,0},{1,9},{9,1},{2,10},{10,2},{3,11},{11,3},{4,12},{12,4},... | collective-permute-start | bytes 4718600 | tf_op jit(solution)/shard_map/ppermute | solution.py:205
  285.4 28.4 %collective-permute-start.35 = (bf16[2,4,8,48,256]{4,3,2,1,0:T(8,128)(2,1)S(1)}, bf16[2,4,8,48,256]{4,3,2,1,0:T(8,128)(2,1)S(1)}, u32[]{:S(2)}, u32[]{:S(2)}) collective-permute-start(bf16[2,4,8,48,256]{4,3,2,1,0:T(8,128)(2,1)S(1)} %pad_maximum_fusion.1), channel_id=1, source_target_pairs={{0,8},{8,0},{1,9},{9,1},{2,10},{10,2},{3,11},{11,3},{4,12},{12,4},... | collective-permute-start | bytes 4718600 | tf_op jit(solution)/shard_map/ppermute | solution.py:205
  290.1 11.3 %collective-permute-start.47 = (bf16[2,4,8,48,256]{4,3,2,1,0:T(8,128)(2,1)S(1)}, bf16[2,4,8,48,256]{4,3,2,1,0:T(8,128)(2,1)S(1)}, u32[]{:S(2)}, u32[]{:S(2)}) collective-permute-start(bf16[2,4,8,48,256]{4,3,2,1,0:T(8,128)(2,1)S(1)} %pad_maximum_fusion.3), channel_id=1, source_target_pairs={{0,8},{8,0},{1,9},{9,1},{2,10},{10,2},{3,11},{11,3},{4,12},{12,4},... | collective-permute-start | bytes 4718600 | tf_op jit(solution)/shard_map/ppermute | solution.py:205
  298.6 21.4 %collective-permute-start.29 = (bf16[2,4,8,48,256]{4,3,2,1,0:T(8,128)(2,1)S(1)}, bf16[2,4,8,48,256]{4,3,2,1,0:T(8,128)(2,1)S(1)}, u32[]{:S(2)}, u32[]{:S(2)}) collective-permute-start(bf16[2,4,8,48,256]{4,3,2,1,0:T(8,128)(2,1)S(1)} %get-tuple-element.66), channel_id=1, source_target_pairs={{0,8},{8,0},{1,9},{9,1},{2,10},{10,2},{3,11},{11,3},{4,12},{12,4},... | collective-permute-start | bytes 4718600 | tf_op jit(solution)/shard_map/ppermute | solution.py:205
  (10 other events, 59.5 us)
